TPU v7x, 512 devices: a whole 4x4x16 slice. The times are simulated.
512 devices in a mesh: ctx: 64 (over z, x), head: 8 (over y, core).
Axes of the slice: x: 4, y: 4, z: 16, core: 2. Of those that a mesh axis runs over, the one named last changes fastest.
Arguments:
- queries: float32 [32768, 2048], P('ctx', 'head'), may hold values from -1024 to 1024
- keys: float32 [32768, 128], P('ctx'), may hold values from -1024 to 1024
- values: float32 [32768, 128], P('ctx'), may hold values from -6 to 6
- cotangent: float32 [32768, 2048], P('ctx', 'head'), may hold values from -384 to 384
- source_ids: int32 [32768], P('ctx'), may hold values from 0 to 63
- source_weights: float32 [64], replicated, may hold values from 0.25 to 4
- q_feature: float32 [16, 128, 128], P('head'), may hold values from -4 to 4
- k_feature: float32 [128, 128], replicated, may hold values from -4 to 4
Outputs:
- grad_queries: float32 [32768, 2048], P('ctx', 'head')
- grad_keys: float32 [32768, 128], P(('ctx', 'head'))
- grad_values: float32 [32768, 128], P(('ctx', 'head'))
- grad_q_feature: float32 [16, 128, 128], P('head')
- grad_k_feature: float32 [128, 128], replicated
All inputs are finite; a program needn't handle non-finite values.
Results may differ from a plain program's by a relative error of at most 0.0015.
Values sent between devices are 32-bit elements; how exact they have to be, the bound alone decides.
A program may use at most 64 MiB of HBM per device.

v0:
```python
import jax
import jax.numpy as jnp
from jax import lax
from jax.sharding import PartitionSpec as P


def entering(value, axis, join, neutral, backward):
    count, mine = (lax.axis_size(axis), lax.axis_index(axis))
    pieces = jax.tree.map(lambda part: lax.all_gather(part, axis), value)
    if backward:
        pieces = jax.tree.map(lambda part: part[::-1], pieces)
        mine = count - 1 - mine
    total = jax.tree.map(
        lambda part, zero: jnp.full_like(part, 0) + jnp.asarray(zero, part.dtype), value, neutral
    )

    def turn(position, total):
        longer = join(total, jax.tree.map(lambda part: part[position], pieces))
        return jax.tree.map(lambda new, old: jnp.where(position < mine, new, old), longer, total)

    return lax.fori_loop(0, count - 1, turn, total)


def matmul(left, right):
    return jnp.dot(left, right, precision=lax.Precision.HIGHEST, preferred_element_type=jnp.float32)


def product(form, left, right):
    return jnp.einsum(
        form, left, right, precision=lax.Precision.HIGHEST, preferred_element_type=jnp.float32
    )


def feature_map(inputs, weight):
    logits = matmul(inputs, weight)
    upper = jax.nn.softmax(logits, axis=-1)
    lower = jax.nn.softmax(-logits, axis=-1)
    return (jnp.concatenate([upper, lower], axis=-1), upper, lower)


def feature_back(inputs, weight, upper, lower, grad_feat):
    half = upper.shape[-1]
    grad_upper = grad_feat[:, :half]
    grad_lower = grad_feat[:, half:]
    grad_logits = upper * (grad_upper - jnp.sum(upper * grad_upper, axis=-1, keepdims=True))
    grad_logits = grad_logits - lower * (
        grad_lower - jnp.sum(lower * grad_lower, axis=-1, keepdims=True)
    )
    return (matmul(grad_logits, weight.T), matmul(inputs.T, grad_logits))


def causal_mask(count):
    row_index = lax.broadcasted_iota(jnp.int32, (count, count), 0)
    col_index = lax.broadcasted_iota(jnp.int32, (count, count), 1)
    return (row_index >= col_index).astype(jnp.float32)


def add_pair(earlier, later):
    return (earlier[0] + later[0], earlier[1] + later[1])


def block_terms(query_c, key_c, value_c, scaled_c, prefix, prefix_tot):
    lower_mask = causal_mask(query_c.shape[1])
    scores = product("ncf,ndf->ncd", query_c, key_c) * lower_mask
    numerator = product("ncd,nde->nce", scores, value_c) + product("ncf,nfe->nce", query_c, prefix)
    normalizer = jnp.sum(scores, axis=2) + product("ncf,nf->nc", query_c, prefix_tot)
    output = numerator / normalizer[..., None]
    grad_numer = scaled_c / normalizer[..., None]
    grad_norm = -jnp.sum(scaled_c * output, axis=2) / normalizer
    grad_scores = (product("nce,nde->ncd", grad_numer, value_c) + grad_norm[..., None]) * lower_mask
    grad_query = (
        product("ncd,ndf->ncf", grad_scores, key_c)
        + product("nce,nfe->ncf", grad_numer, prefix)
        + grad_norm[..., None] * prefix_tot[:, None, :]
    )
    grad_key = product("ncd,ncf->ndf", grad_scores, query_c)
    grad_value = product("ncd,nce->nde", scores, grad_numer)
    carried = product("ncf,nce->nfe", query_c, grad_numer)
    carried_totals = product("nc,ncf->nf", grad_norm, query_c)
    return (grad_query, grad_key, grad_value, carried, carried_totals)


def on_device(queries, keys, values, cotangent, source_ids, source_weights, q_feature, k_feature):
    head_count = q_feature.shape[0]
    width = q_feature.shape[1]
    features = 2 * q_feature.shape[2]
    rows = queries.shape[0]
    piece = min(128, rows)
    pieces = rows // piece
    source_index = lax.broadcasted_iota(jnp.int32, (1, source_weights.shape[0]), 1)
    lookup = (source_ids[:, None] == source_index).astype(jnp.float32)
    weight = jnp.sum(lookup * source_weights[None, :], axis=1)
    key_feat, key_upper, key_lower = feature_map(keys, k_feature)
    key_c = key_feat.reshape(pieces, piece, features)
    value_c = values.reshape(pieces, piece, width)
    piece_state = product("ncf,nce->nfe", key_c, value_c)
    piece_tot = jnp.sum(key_c, axis=1)
    whole_local = (jnp.sum(piece_state, axis=0), jnp.sum(piece_tot, axis=0))
    whole_zero = (jnp.zeros((features, width), jnp.float32), jnp.zeros((features,), jnp.float32))
    earlier, earlier_totals = entering(
        (whole_local[0], whole_local[1]), "ctx", add_pair, whole_zero, False
    )
    prefix = jnp.cumsum(piece_state, axis=0) - piece_state + earlier[None]
    prefix_tot = jnp.cumsum(piece_tot, axis=0) - piece_tot + earlier_totals[None]
    grad_keyfeat = jnp.zeros(key_feat.shape, jnp.float32)
    grad_vals = jnp.zeros(values.shape, jnp.float32)
    piece_carried = jnp.zeros((pieces, features, width), jnp.float32)
    piece_carried_tot = jnp.zeros((pieces, features), jnp.float32)
    query_grads = []
    weight_grads = []
    for head in range(head_count):
        query_head = queries[:, head * width : (head + 1) * width]
        query_feat, query_upper, query_lower = feature_map(query_head, q_feature[head])
        scaled = cotangent[:, head * width : (head + 1) * width] * weight[:, None]
        grad_query, grad_key, grad_value, carried, carried_totals = block_terms(
            query_feat.reshape(pieces, piece, features),
            key_c,
            value_c,
            scaled.reshape(pieces, piece, width),
            prefix,
            prefix_tot,
        )
        grad_head, grad_weight = feature_back(
            query_head,
            q_feature[head],
            query_upper,
            query_lower,
            grad_query.reshape(rows, features),
        )
        query_grads.append(grad_head)
        weight_grads.append(grad_weight)
        grad_keyfeat = grad_keyfeat + grad_key.reshape(rows, features)
        grad_vals = grad_vals + grad_value.reshape(rows, width)
        piece_carried = piece_carried + carried
        piece_carried_tot = piece_carried_tot + carried_totals
    carried_all = jnp.sum(piece_carried, axis=0)
    carried_tot = jnp.sum(piece_carried_tot, axis=0)
    inner_later = carried_all[None] - jnp.cumsum(piece_carried, axis=0)
    inner_tot = carried_tot[None] - jnp.cumsum(piece_carried_tot, axis=0)
    grad_keyfeat = grad_keyfeat + (
        product("nce,nfe->ncf", value_c, inner_later) + inner_tot[:, None, :]
    ).reshape(rows, features)
    grad_vals = grad_vals + product("ncf,nfe->nce", key_c, inner_later).reshape(rows, width)
    later, later_tot = entering((carried_all, carried_tot), "ctx", add_pair, whole_zero, True)
    grad_keyfeat = grad_keyfeat + matmul(values, later.T) + later_tot[None, :]
    grad_vals = grad_vals + matmul(key_feat, later)
    grad_key_part, grad_kweight = feature_back(keys, k_feature, key_upper, key_lower, grad_keyfeat)
    grad_keys, grad_values = (
        lax.psum_scatter(grad_key_part, "head", scatter_dimension=0, tiled=True),
        lax.psum_scatter(grad_vals, "head", scatter_dimension=0, tiled=True),
    )
    grad_qweight = lax.psum(jnp.stack(weight_grads, axis=0), "ctx")
    grad_kweight = lax.psum(grad_kweight, ("ctx", "head"))
    return (
        jnp.concatenate(query_grads, axis=1),
        grad_keys,
        grad_values,
        grad_qweight,
        grad_kweight,
    )


def solution(mesh):
    placed = (
        P("ctx", "head"),
        P("ctx", None),
        P("ctx", None),
        P("ctx", "head"),
        P("ctx"),
        P(),
        P("head", None, None),
        P(),
    )
    return jax.shard_map(
        on_device,
        mesh=mesh,
        in_specs=placed,
        out_specs=(
            P("ctx", "head"),
            P(("ctx", "head"), None),
            P(("ctx", "head"), None),
            P("head", None, None),
            P(),
        ),
        check_vma=False,
    )
```

profile of v0, /device:TPU:2, one launch (start us, length us, event | category | flops | bytes accessed | tf_op | source)
XLA Modules:
  0.0 1215.9 jit_solution(13639607046449780209)
XLA Ops:
  7.2 1.5 fusion.97
  9.8 2.1 fusion.103
  14.9 87.9 %all-gather.4 = f32[64,1,256]{2,1,0:T(1,128)S(1)} all-gather(f32[1,1,256]{2,1,0:T(1,128)S(1)} %bitcast.226), channel_id=3, replica_groups=mesh['ctx'=64,'head'=8] {'ctx'}, dimensions={0}, use_global_device_ids=true | all-gather | bytes 66560 | tf_op jit(solution)/shard_map/all_gather | solution.py:9
  106.6 1.8 fusion.102
  108.4 1.8 fusion.104
  110.2 62.4 %all-gather.9.cloned.1.call-done = f32[16384,128]{1,0:T(8,128)} async-done(((f32[256,128]{1,0:T(8,128)}), f32[16384,128]{1,0:T(8,128)}) %all-gather.9.cloned.1.call-update) | async-done | bytes 8388624 | tf_op jit(solution)/shard_map/all_gather | solution.py:9
  172.6 106.3 %while.32 = (s32[]{:T(128)}, f32[256,128]{1,0:T(8,128)S(1)}, f32[256]{0:T(256)S(1)}, s32[]{:T(128)}, f32[64,256,128]{2,1,0:T(8,128)}, /*index=5*/f32[64,256]{1,0:T(8,128)}, s32[]{:T(128)}, s32[]{:T(128)}) while((s32[]{:T(128)}, f32[256,128]{1,0:T(8,128)S(1)}, f32[256]{0:T(256)S(1)}, s32[]{:T(128)}, f32[64,256,128]{2,1,0:T(8,128)}, ...), condition=%wide.region_15.16_spmd.clone, body=%wide.region_14.15_spmd.clone.sunk | while | flops 99076 | bytes 398459 | solution.py:21
  280.5 2.1 fusion.105
  285.3 1.6 fusion.14
  287.9 1.6 fusion.15
  290.7 80.2 %all-gather.5 = f32[64,1,256]{2,1,0:T(1,128)S(1)} all-gather(f32[1,1,256]{2,1,0:T(1,128)S(1)} %bitcast.225), channel_id=5, replica_groups=mesh['ctx'=64,'head'=8] {'ctx'}, dimensions={0}, use_global_device_ids=true | all-gather | bytes 66560 | tf_op jit(solution)/shard_map/all_gather | solution.py:9
  374.8 1.8 copy.214
  376.6 1.8 copy.215
  381.2 1.6 fusion.6
  385.1 1.5 fusion.44
  387.7 1.5 convolution_add_fusion.2
  389.3 1.4 fusion.4
  390.7 2.0 copy.209
  392.7 1.8 copy.213
  396.7 1.4 convolution_bitcast_fusion.2
  402.3 1.7 fusion.93
  405.1 1.6 fusion.7
  406.8 27.8 %all-gather.11.cloned.1.call-done = f32[16384,128]{1,0:T(8,128)} async-done(((f32[256,128]{1,0:T(8,128)}), f32[16384,128]{1,0:T(8,128)}) %all-gather.11.cloned.1.call-update) | async-done | bytes 8388624 | tf_op jit(solution)/shard_map/all_gather | solution.py:9
  434.6 7.7 rev.6
  442.2 106.4 %while.33 = (s32[]{:T(128)}, f32[256,128]{1,0:T(8,128)S(1)}, f32[256]{0:T(256)S(1)}, s32[]{:T(128)}, f32[64,256,128]{2,1,0:T(8,128)}, /*index=5*/f32[64,256]{1,0:T(8,128)}, s32[]{:T(128)}, s32[]{:T(128)}) while((s32[]{:T(128)}, f32[256,128]{1,0:T(8,128)S(1)}, f32[256]{0:T(256)S(1)}, s32[]{:T(128)}, f32[64,256,128]{2,1,0:T(8,128)}, ...), condition=%wide.region_33.34_spmd.clone, body=%wide.region_32.33_spmd.clone.sunk | while | flops 99076 | bytes 398459 | solution.py:21
  550.8 1.7 convolution_add_fusion.5
  555.7 138.0 %all-reduce.3.cloned.1.call-done = f32[2,128,128]{1,2,0:T(8,128)} async-done(((f32[2,128,128]{1,2,0:T(8,128)}), f32[2,128,128]{1,2,0:T(8,128)}) %all-reduce.3.cloned.1.call-update) | async-done | bytes 131088 | tf_op jit(solution)/shard_map/psum | solution.py:152
  693.8 1.7 copy.181
  695.4 440.1 %all-reduce.5.cloned.1.call-done = f32[128,128]{0,1:T(8,128)} async-done(((f32[128,128]{0,1:T(8,128)}), f32[128,128]{0,1:T(8,128)}) %all-reduce.5.cloned.1.call-update) | async-done | bytes 65552 | tf_op jit(solution)/shard_map/psum | solution.py:153
  1135.6 1.6 copy.182
  1137.1 31.7 %reduce-scatter.5.cloned.1.call-done = f32[64,128]{1,0:T(8,128)} async-done(((f32[512,128]{1,0:T(8,128)}), f32[64,128]{1,0:T(8,128)}) %reduce-scatter.5.cloned.1.call-update) | async-done | bytes 32784 | tf_op jit(solution)/shard_map/reduce_scatter | solution.py:150
  1168.8 40.2 %reduce-scatter.3.cloned.1.call-done = f32[64,128]{1,0:T(8,128)} async-done(((f32[512,128]{1,0:T(8,128)}), f32[64,128]{1,0:T(8,128)}) %reduce-scatter.3.cloned.1.call-update) | async-done | bytes 32784 | tf_op jit(solution)/shard_map/reduce_scatter | solution.py:149
  (489 shorter events, 246.5 us)
Async XLA Ops:
  7.2 2.6 copy-start
  7.2 98.1 %copy-start.12 = (f32[2,128,128]{2,1,0:T(8,128)S(1)}, f32[2,128,128]{2,1,0:T(8,128)}, u32[]{:S(2)}) copy-start(f32[2,128,128]{2,1,0:T(8,128)} %param.18) | copy-start | bytes 393220
  7.2 98.1 %copy-start.4 = (f32[512,256]{1,0:T(8,128)S(1)}, f32[512,256]{1,0:T(8,128)}, u32[]{:S(2)}) copy-start(f32[512,256]{1,0:T(8,128)} %param.12) | copy-start | bytes 1572868
  7.2 165.4 %all-gather.9.cloned.1.call-start = ((), (), s32[]{:S(2)}) async-start(), calls=%async_computation.6 | async-start | bytes 8519680 | tf_op jit(solution)/shard_map/all_gather | solution.py:9
  11.9 422.7 %all-gather.11.cloned.1.call-start = ((), (), s32[]{:S(2)}) async-start(), calls=%async_computation.7 | async-start | bytes 8519680 | tf_op jit(solution)/shard_map/all_gather | solution.py:9
  105.1 174.8 %copy-start.8 = (f32[4,128,128]{1,2,0:T(8,128)S(1)}, f32[4,128,128]{1,2,0:T(8,128)}, u32[]{:S(2)}) copy-start(f32[4,128,128]{1,2,0:T(8,128)} %copy.142) | copy-start | bytes 786436
  105.3 173.6 %copy-start.10 = (f32[128,128]{0,1:T(8,128)}, f32[128,128]{0,1:T(8,128)S(1)}, u32[]{:S(2)}) copy-start(f32[128,128]{0,1:T(8,128)S(1)} %fusion.88) | copy-start | bytes 196612
  279.0 92.5 %copy-start.11 = (f32[128,128]{0,1:T(8,128)S(1)}, f32[128,128]{0,1:T(8,128)}, u32[]{:S(2)}) copy-start(f32[128,128]{0,1:T(8,128)} %copy-done.10) | copy-start | bytes 196612
  282.6 411.2 %all-reduce.3.cloned.1.call-start = ((), (), s32[]{:S(2)}) async-start(), calls=%async_computation.4 | async-start | bytes 262144 | tf_op jit(solution)/shard_map/psum | solution.py:152
  290.6 90.5 %copy-start.15 = (f32[256]{0:T(256)}, f32[256]{0:T(256)S(1)}, u32[]{:S(2)}) copy-start(f32[256]{0:T(256)S(1)} %get-tuple-element.329) | copy-start | bytes 3076
  372.0 0.7 copy-start.6
  379.8 0.7 copy-start.7
  382.8 11.8 copy-start.3
  396.6 3.7 copy-start.1
  406.7 728.8 %all-reduce.5.cloned.1.call-start = ((), (), s32[]{:S(2)}) async-start(), calls=%async_computation.5 | async-start | bytes 131072 | tf_op jit(solution)/shard_map/psum | solution.py:153
  434.6 114.1 %copy-start.5 = (f32[512,256]{0,1:T(8,128)S(1)}, f32[512,256]{0,1:T(8,128)}, u32[]{:S(2)}) copy-start(f32[512,256]{0,1:T(8,128)} %copy.209) | copy-start | bytes 1572868
  434.6 114.9 %copy-start.9 = (f32[512,128]{1,0:T(8,128)S(1)}, f32[512,128]{1,0:T(8,128)}, u32[]{:S(2)}) copy-start(f32[512,128]{1,0:T(8,128)} %param.13) | copy-start | bytes 786436
  434.6 118.0 %copy-start.14 = (f32[128,128]{1,0:T(8,128)S(1)}, f32[128,128]{1,0:T(8,128)}, u32[]{:S(2)}) copy-start(f32[128,128]{1,0:T(8,128)} %param.19) | copy-start | bytes 196612
  442.2 111.6 %copy-start.2 = (f32[512,128]{0,1:T(8,128)S(1)}, f32[512,128]{0,1:T(8,128)}, u32[]{:S(2)}) copy-start(f32[512,128]{0,1:T(8,128)} %copy-done.1) | copy-start | bytes 786436
  442.2 111.6 %copy-start.13 = (f32[2,128,128]{2,1,0:T(8,128)S(1)}, f32[2,128,128]{2,1,0:T(8,128)}, u32[]{:S(2)}) copy-start(f32[2,128,128]{2,1,0:T(8,128)} %param.18) | copy-start | bytes 393220
  550.5 618.3 %reduce-scatter.5.cloned.1.call-start = ((), (), s32[]{:S(2)}) async-start(), calls=%async_computation.3 | async-start | bytes 294912 | tf_op jit(solution)/shard_map/reduce_scatter | solution.py:150
  552.5 656.5 %reduce-scatter.3.cloned.1.call-start = ((), (), s32[]{:S(2)}) async-start(), calls=%async_computation.2 | async-start | bytes 294912 | tf_op jit(solution)/shard_map/reduce_scatter | solution.py:149
Sparse Core Ops, SparseCore 0:
  12.0 160.5 all-gather.8
  282.7 151.7 all-gather.10
  438.0 255.7 all-reduce.2
  699.7 435.8 all-reduce.4
  1139.0 29.7 reduce-scatter.4
  1172.0 36.9 reduce-scatter.2
where the time goes:
time: 1220 us
  waiting for transfers between devices  740 us (61%)
  blocking collectives  168 us (14%)
  other arithmetic  133 us (11%)
  local copies, waits for them, and re-layouts  116 us (10%)
  matrix products  40.1 us (3%)
  between operations  14.6 us (1%)
    psum x1, waiting for transfers between devices, on_device(): grad_kweight = lax.psum(grad_kweight, ('ctx', 'head'))  440 us
    all_gather x2, blocking collectives, entering(): pieces = jax.tree.map(lambda part: lax.all_gather(part, axis), value)  168 us
    psum x1, waiting for transfers between devices, on_device(): grad_qweight = lax.psum(jnp.stack(weight_grads, axis=0), 'ctx')  138 us
    select_n x252, other arithmetic, turn(): jnp.where(position < mine, new, old)  121 us
    all_gather x2, waiting for transfers between devices, entering(): pieces = jax.tree.map(lambda part: lax.all_gather(part, axis), value)  90.2 us
    dynamic_slice x126, local copies, waits for them, and re-layouts, turn(): longer = join(total, jax.tree.map(lambda part: part[position], pieces))  89 us
    reduce_scatter x1, waiting for transfers between devices, on_device(): lax.psum_scatter(grad_key_part, 'head', scatter_dimension=0, tiled=True)  40.2 us
    reduce_scatter x1, waiting for transfers between devices, on_device(): lax.psum_scatter(grad_vals, 'head', scatter_dimension=0, tiled=True)  31.7 us
  transfers between devices with their start and end apart: 6, of which 6 were waited for; matrix products, arithmetic and copies ran while one was open for 14% of the time, Pallas kernels for 0%

commit v1 on v0

--- a/solution.py
+++ b/solution.py
@@ -150,7 +150,7 @@
         lax.psum_scatter(grad_vals, "head", scatter_dimension=0, tiled=True),
     )
     grad_qweight = lax.psum(jnp.stack(weight_grads, axis=0), "ctx")
-    grad_kweight = lax.psum(grad_kweight, ("ctx", "head"))
+    grad_kweight = lax.psum(lax.psum(grad_kweight, "head"), "ctx")
     return (
         jnp.concatenate(query_grads, axis=1),
         grad_keys,

time: 1220 us -> 978 us (0.80)
  waiting for transfers between devices: 740 us -> 494 us
    psum x1, waiting for transfers between devices: 440 us -> 69.6 us  [on_device(): grad_kweight = lax.psum(lax.psum(grad_kweight, 'head'), 'ctx')]
    psum x1, waiting for transfers between devices: 138 us -> 260 us  [on_device(): grad_qweight = lax.psum(jnp.stack(weight_grads, axis=0), 'ctx')]
  transfers between devices with their start and end apart: 6 -> 6, of which waited for: 6 -> 6; matrix products, arithmetic and copies ran while one was open for 14% -> 6% of each run, Pallas kernels for 0% -> 0%
where the time goes in v1:
time: 978 us; the launch traced here: 970 us
  waiting for transfers between devices  494 us (51%)
  blocking collectives  168 us (17%)
  other arithmetic  133 us (14%)
  local copies, waits for them, and re-layouts  116 us (12%)
  matrix products  40.2 us (4%)
  between operations  14.6 us (1%)
    psum x1, waiting for transfers between devices, on_device(): grad_qweight = lax.psum(jnp.stack(weight_grads, axis=0), 'ctx')  260 us
    all_gather x2, blocking collectives, entering(): pieces = jax.tree.map(lambda part: lax.all_gather(part, axis), value)  168 us
    select_n x252, other arithmetic, turn(): jnp.where(position < mine, new, old)  121 us
    all_gather x2, waiting for transfers between devices, entering(): pieces = jax.tree.map(lambda part: lax.all_gather(part, axis), value)  90.9 us
    dynamic_slice x126, local copies, waits for them, and re-layouts, turn(): longer = join(total, jax.tree.map(lambda part: part[position], pieces))  89 us
    psum x1, waiting for transfers between devices, on_device(): grad_kweight = lax.psum(lax.psum(grad_kweight, 'head'), 'ctx')  69.6 us
    reduce_scatter x1, waiting for transfers between devices, on_device(): lax.psum_scatter(grad_key_part, 'head', scatter_dimension=0, tiled=True)  40.6 us
    reduce_scatter x1, waiting for transfers between devices, on_device(): lax.psum_scatter(grad_vals, 'head', scatter_dimension=0, tiled=True)  33.2 us
  transfers between devices with their start and end apart: 6, of which 6 were waited for; matrix products, arithmetic and copies ran while one was open for 6% of the time, Pallas kernels for 0%

profile of v1, /device:TPU:2, one launch (start us, length us, event | category | flops | bytes accessed | tf_op | source)
XLA Modules:
  0.0 969.5 jit_solution(3737522410225893496)
XLA Ops:
  7.2 1.5 fusion.97
  9.8 2.1 fusion.103
  14.9 87.9 %all-gather.4 = f32[64,1,256]{2,1,0:T(1,128)S(1)} all-gather(f32[1,1,256]{2,1,0:T(1,128)S(1)} %bitcast.226), channel_id=3, replica_groups=mesh['ctx'=64,'head'=8] {'ctx'}, dimensions={0}, use_global_device_ids=true | all-gather | bytes 66560 | tf_op jit(solution)/shard_map/all_gather | solution.py:9
  106.6 1.8 fusion.102
  108.4 1.8 fusion.104
  110.2 62.4 %all-gather.9.cloned.1.call-done = f32[16384,128]{1,0:T(8,128)} async-done(((f32[256,128]{1,0:T(8,128)}), f32[16384,128]{1,0:T(8,128)}) %all-gather.9.cloned.1.call-update) | async-done | bytes 8388624 | tf_op jit(solution)/shard_map/all_gather | solution.py:9
  172.6 106.3 %while.32 = (s32[]{:T(128)}, f32[256,128]{1,0:T(8,128)S(1)}, f32[256]{0:T(256)S(1)}, s32[]{:T(128)}, f32[64,256,128]{2,1,0:T(8,128)}, /*index=5*/f32[64,256]{1,0:T(8,128)}, s32[]{:T(128)}, s32[]{:T(128)}) while((s32[]{:T(128)}, f32[256,128]{1,0:T(8,128)S(1)}, f32[256]{0:T(256)S(1)}, s32[]{:T(128)}, f32[64,256,128]{2,1,0:T(8,128)}, ...), condition=%wide.region_15.16_spmd.clone, body=%wide.region_14.15_spmd.clone.sunk | while | flops 99076 | bytes 398459 | solution.py:21
  280.5 2.1 fusion.105
  285.3 1.6 fusion.14
  287.9 1.6 fusion.15
  290.7 80.2 %all-gather.5 = f32[64,1,256]{2,1,0:T(1,128)S(1)} all-gather(f32[1,1,256]{2,1,0:T(1,128)S(1)} %bitcast.225), channel_id=5, replica_groups=mesh['ctx'=64,'head'=8] {'ctx'}, dimensions={0}, use_global_device_ids=true | all-gather | bytes 66560 | tf_op jit(solution)/shard_map/all_gather | solution.py:9
  374.8 1.8 copy.214
  376.6 1.8 copy.215
  381.2 1.6 fusion.6
  385.1 1.5 fusion.44
  387.7 1.5 convolution_add_fusion.2
  389.3 1.4 fusion.4
  390.7 2.0 copy.209
  392.7 1.8 copy.213
  396.7 1.4 convolution_bitcast_fusion.2
  401.7 1.7 fusion.93
  404.4 1.6 fusion.7
  406.1 28.5 %all-gather.11.cloned.1.call-done = f32[16384,128]{1,0:T(8,128)} async-done(((f32[256,128]{1,0:T(8,128)}), f32[16384,128]{1,0:T(8,128)}) %all-gather.11.cloned.1.call-update) | async-done | bytes 8388624 | tf_op jit(solution)/shard_map/all_gather | solution.py:9
  434.6 7.7 rev.6
  442.2 106.4 %while.33 = (s32[]{:T(128)}, f32[256,128]{1,0:T(8,128)S(1)}, f32[256]{0:T(256)S(1)}, s32[]{:T(128)}, f32[64,256,128]{2,1,0:T(8,128)}, /*index=5*/f32[64,256]{1,0:T(8,128)}, s32[]{:T(128)}, s32[]{:T(128)}) while((s32[]{:T(128)}, f32[256,128]{1,0:T(8,128)S(1)}, f32[256]{0:T(256)S(1)}, s32[]{:T(128)}, f32[64,256,128]{2,1,0:T(8,128)}, ...), condition=%wide.region_33.34_spmd.clone, body=%wide.region_32.33_spmd.clone.sunk | while | flops 99076 | bytes 398459 | solution.py:21
  551.2 69.6 %all-reduce.4.cloned.1.call-done = f32[128,128]{0,1:T(8,128)} async-done(((f32[128,128]{0,1:T(8,128)}), f32[128,128]{0,1:T(8,128)}) %all-reduce.4.cloned.1.call-update) | async-done | bytes 65552 | tf_op jit(solution)/shard_map/psum | solution.py:153
  621.1 1.7 convolution_add_fusion.5
  626.1 259.6 %all-reduce.6.cloned.1.call-done = (f32[2,128,128]{1,2,0:T(8,128)}, f32[128,128]{0,1:T(8,128)}) async-done(((f32[2,128,128]{1,2,0:T(8,128)}, f32[128,128]{0,1:T(8,128)}), (f32[2,128,128]{1,2,0:T(8,128)}, f32[128,128]{0,1:T(8,128)})) %all-reduce.6.cloned.1.call-update) | async-done | bytes 196624 | tf_op jit(solution)/shard_map/psum | solution.py:152
  885.7 1.7 copy.181
  887.4 1.6 copy.182
  888.9 33.2 %reduce-scatter.5.cloned.1.call-done = f32[64,128]{1,0:T(8,128)} async-done(((f32[512,128]{1,0:T(8,128)}), f32[64,128]{1,0:T(8,128)}) %reduce-scatter.5.cloned.1.call-update) | async-done | bytes 32784 | tf_op jit(solution)/shard_map/reduce_scatter | solution.py:150
  922.1 40.6 %reduce-scatter.3.cloned.1.call-done = f32[64,128]{1,0:T(8,128)} async-done(((f32[512,128]{1,0:T(8,128)}), f32[64,128]{1,0:T(8,128)}) %reduce-scatter.3.cloned.1.call-update) | async-done | bytes 32784 | tf_op jit(solution)/shard_map/reduce_scatter | solution.py:149
  (489 shorter events, 246.6 us)
Async XLA Ops:
  7.2 2.6 copy-start
  7.2 98.1 %copy-start.12 = (f32[2,128,128]{2,1,0:T(8,128)S(1)}, f32[2,128,128]{2,1,0:T(8,128)}, u32[]{:S(2)}) copy-start(f32[2,128,128]{2,1,0:T(8,128)} %param.18) | copy-start | bytes 393220
  7.2 98.1 %copy-start.4 = (f32[512,256]{1,0:T(8,128)S(1)}, f32[512,256]{1,0:T(8,128)}, u32[]{:S(2)}) copy-start(f32[512,256]{1,0:T(8,128)} %param.12) | copy-start | bytes 1572868
  7.2 165.4 %all-gather.9.cloned.1.call-start = ((), (), s32[]{:S(2)}) async-start(), calls=%async_computation.5 | async-start | bytes 8519680 | tf_op jit(solution)/shard_map/all_gather | solution.py:9
  11.9 422.6 %all-gather.11.cloned.1.call-start = ((), (), s32[]{:S(2)}) async-start(), calls=%async_computation.6 | async-start | bytes 8519680 | tf_op jit(solution)/shard_map/all_gather | solution.py:9
  105.1 174.8 %copy-start.8 = (f32[4,128,128]{1,2,0:T(8,128)S(1)}, f32[4,128,128]{1,2,0:T(8,128)}, u32[]{:S(2)}) copy-start(f32[4,128,128]{1,2,0:T(8,128)} %copy.142) | copy-start | bytes 786436
  105.3 173.6 %copy-start.10 = (f32[128,128]{0,1:T(8,128)}, f32[128,128]{0,1:T(8,128)S(1)}, u32[]{:S(2)}) copy-start(f32[128,128]{0,1:T(8,128)S(1)} %fusion.88) | copy-start | bytes 196612
  279.0 92.5 %copy-start.11 = (f32[128,128]{0,1:T(8,128)S(1)}, f32[128,128]{0,1:T(8,128)}, u32[]{:S(2)}) copy-start(f32[128,128]{0,1:T(8,128)} %copy-done.10) | copy-start | bytes 196612
  282.6 338.2 %all-reduce.4.cloned.1.call-start = ((), (), s32[]{:S(2)}) async-start(), calls=%async_computation.4 | async-start | bytes 131072 | tf_op jit(solution)/shard_map/psum | solution.py:153
  290.6 90.5 %copy-start.15 = (f32[256]{0:T(256)}, f32[256]{0:T(256)S(1)}, u32[]{:S(2)}) copy-start(f32[256]{0:T(256)S(1)} %get-tuple-element.331) | copy-start | bytes 3076
  372.0 0.7 copy-start.6
  379.8 0.7 copy-start.7
  382.8 11.8 %copy-start.3 = (f32[512,128]{0,1:T(8,128)S(1)}, f32[512,128]{0,1:T(8,128)}, u32[]{:S(2)}) copy-start(f32[512,128]{0,1:T(8,128)} %copy.214) | copy-start | bytes 786436
  396.6 7.8 copy-start.1
  434.6 114.0 %copy-start.5 = (f32[512,256]{0,1:T(8,128)S(1)}, f32[512,256]{0,1:T(8,128)}, u32[]{:S(2)}) copy-start(f32[512,256]{0,1:T(8,128)} %copy.209) | copy-start | bytes 1572868
  434.6 114.9 %copy-start.9 = (f32[512,128]{1,0:T(8,128)S(1)}, f32[512,128]{1,0:T(8,128)}, u32[]{:S(2)}) copy-start(f32[512,128]{1,0:T(8,128)} %param.13) | copy-start | bytes 786436
  442.2 180.7 %copy-start.14 = (f32[128,128]{1,0:T(8,128)S(1)}, f32[128,128]{1,0:T(8,128)}, u32[]{:S(2)}) copy-start(f32[128,128]{1,0:T(8,128)} %param.19) | copy-start | bytes 196612
  442.2 182.0 %copy-start.2 = (f32[512,128]{0,1:T(8,128)S(1)}, f32[512,128]{0,1:T(8,128)}, u32[]{:S(2)}) copy-start(f32[512,128]{0,1:T(8,128)} %copy-done.1) | copy-start | bytes 786436
  442.2 182.0 %copy-start.13 = (f32[2,128,128]{2,1,0:T(8,128)S(1)}, f32[2,128,128]{2,1,0:T(8,128)}, u32[]{:S(2)}) copy-start(f32[2,128,128]{2,1,0:T(8,128)} %param.18) | copy-start | bytes 393220
  550.5 335.2 %all-reduce.6.cloned.1.call-start = ((), (), s32[]{:S(2)}) async-start(), calls=%async_computation.7 | async-start | bytes 393216 | tf_op jit(solution)/shard_map/psum | solution.py:152
  620.9 301.2 %reduce-scatter.5.cloned.1.call-start = ((), (), s32[]{:S(2)}) async-start(), calls=%async_computation.3 | async-start | bytes 294912 | tf_op jit(solution)/shard_map/reduce_scatter | solution.py:150
  622.9 339.8 %reduce-scatter.3.cloned.1.call-start = ((), (), s32[]{:S(2)}) async-start(), calls=%async_computation.2 | async-start | bytes 294912 | tf_op jit(solution)/shard_map/reduce_scatter | solution.py:149
Sparse Core Ops, SparseCore 0:
  12.0 160.5 all-gather.8
  282.7 151.7 all-gather.10
  550.6 70.1 all-reduce.3
  625.2 260.4 all-reduce.5
  888.9 33.1 reduce-scatter.4
  925.5 37.0 reduce-scatter.2
